TPU v7x, 1024 devices: a whole 4x8x16 slice. The times are simulated.
1024 devices in a mesh: dp: 8 (over y), ctx: 16 (over z), tp: 8 (over x, core).
Axes of the slice: x: 4, y: 8, z: 16, core: 2. Of those that a mesh axis runs over, the one named last changes fastest.
Arguments:
- tokens: bfloat16 [16384, 4096], P(('dp', 'ctx'), 'tp'), parts along dimension 0, may hold values from -6 to 6
- expert_ids: int32 [16384, 8], P(('dp', 'ctx')), parts along dimension 0, may hold values from 0 to 127, all different within a row; in each aligned block of 128 rows (0 to 127, 128 to 255, ...) at most 16 rows name the same one
- route_weight: float32 [16384, 8], P(('dp', 'ctx')), parts along dimension 0, may hold values from 0.1 to 1
- gate_weight: bfloat16 [128, 384, 4096], P(('ctx', 'tp')), may hold values from -0.09375 to 0.09375
- up_weight: bfloat16 [128, 384, 4096], P(('ctx', 'tp')), may hold values from -0.09375 to 0.09375
- down_weight: bfloat16 [128, 384, 4096], P(('ctx', 'tp')), may hold values from -0.15625 to 0.15625
Outputs:
- mixed_out: bfloat16 [16384, 4096], P(('dp', 'ctx'), 'tp'), parts along dimension 0
There are 8 independent parts, one for each index of `dp`. A program takes and returns all parts, laid end to end along the dimension named above; an argument that names none is the same for every part. Nothing has to cross between parts.
Inputs may be any that keep to these rules, and one draw needn't show every extreme that they name: `expert_ids`: each token names 8 different experts. In each aligned block of 128 tokens no expert is named by more than 16 tokens, a bound that some block reaches.
All inputs are finite; a program needn't handle non-finite values.
Results may differ from a plain program's by a relative error of at most 0.018.
Values may be sent and summed in bfloat16 or wider, within the bound.
A program may use at most 128 MiB of HBM per device.

v0:
```python
import jax
import jax.numpy as jnp
from jax import lax
from jax.sharding import PartitionSpec as P

SPLIT = 4
CAP = 16


def shards(tokens, expert_ids, route_weight, gate_weight, up_weight, down_weight):
    tok_rows = tokens.shape[0]
    route_count = expert_ids.shape[1]
    ctx_size = lax.axis_size("ctx")
    tp_size = lax.axis_size("tp")
    groups = tp_size // SPLIT
    exp_window = ctx_size * groups
    capacity = CAP
    whole = lax.all_gather(tokens, "tp", axis=1, tiled=True)
    full_width = whole.shape[1]
    flat_ids = expert_ids.reshape(-1)
    live_route = flat_ids < exp_window
    expert_marks = (flat_ids[:, None] == jnp.arange(exp_window, dtype=jnp.int32)[None, :]).astype(
        jnp.int32
    )
    running = jnp.cumsum(expert_marks, axis=0, dtype=jnp.int32) - 1
    slot_index = jnp.sum(running * expert_marks, axis=1, dtype=jnp.int32)
    target_row = jnp.where(live_route, flat_ids * capacity + slot_index, -1)
    place_index = jnp.arange(exp_window * capacity, dtype=jnp.int32)
    select_mask = (target_row[None, :] == place_index[:, None]).astype(jnp.float32)
    select_mask = select_mask.reshape(exp_window * capacity, tok_rows, route_count)
    pick_all = jnp.sum(select_mask, axis=2).reshape(ctx_size, groups, capacity, tok_rows)
    weight_all = jnp.sum(select_mask * route_weight.reshape(1, tok_rows, route_count), axis=2)
    weight_all = weight_all.reshape(ctx_size, groups, capacity, tok_rows)
    my_group = lax.axis_index("tp") // SPLIT
    pick_mine = (
        jnp.take(pick_all, my_group, axis=1)
        .reshape(ctx_size * capacity, tok_rows)
        .astype(jnp.bfloat16)
    )
    outgoing = jnp.dot(pick_mine, whole, preferred_element_type=jnp.float32).astype(jnp.bfloat16)
    outgoing = outgoing.reshape(ctx_size, capacity, full_width)
    arrived = lax.all_to_all(outgoing, "ctx", split_axis=0, concat_axis=0, tiled=True)
    gate_vals = jnp.einsum(
        "scd,fd->scf", arrived, gate_weight[0], preferred_element_type=jnp.float32
    )
    up_vals = jnp.einsum("scd,fd->scf", arrived, up_weight[0], preferred_element_type=jnp.float32)
    hidden = (jax.nn.silu(gate_vals) * up_vals).astype(jnp.bfloat16)
    part_out = jnp.einsum("scf,fd->scd", hidden, down_weight[0], preferred_element_type=jnp.float32)
    part_out = part_out.astype(jnp.bfloat16)
    back = lax.all_to_all(part_out, "ctx", split_axis=0, concat_axis=0, tiled=True)
    weight_mine = jnp.take(weight_all, my_group, axis=1).reshape(ctx_size * capacity, tok_rows)
    term = jnp.dot(
        weight_mine.T,
        back.reshape(-1, full_width).astype(jnp.float32),
        precision=lax.Precision.HIGHEST,
    )
    mixed_out = lax.psum_scatter(term.astype(jnp.bfloat16), "tp", scatter_dimension=1, tiled=True)
    return mixed_out


def solution(mesh):
    return jax.shard_map(
        shards,
        mesh=mesh,
        in_specs=(
            P(("dp", "ctx"), "tp"),
            P(("dp", "ctx"), None),
            P(("dp", "ctx"), None),
            P(("ctx", "tp"), None, None),
            P(("ctx", "tp"), None, None),
            P(("ctx", "tp"), None, None),
        ),
        out_specs=P(("dp", "ctx"), "tp"),
        check_vma=False,
    )
```

profile of v0, /device:TPU:7, one launch (start us, length us, event | category | flops | bytes accessed | tf_op | source)
XLA Modules:
  0.0 322.2 jit_solution(4986902523206521291)
XLA Ops:
  6.5 0.0 copy-start
  6.5 0.0 all-gather.2.cloned.1.call-start
  6.5 0.7 all-gather.2.cloned.1.call-update
  7.3 0.0 reduce-scatter.2.cloned.1.call-start
  7.3 0.9 copy.29
  8.3 0.1 eq.43
  8.4 0.1 eq.39
  8.5 9.0 %reduce-window.6 = s32[32,8,128]{2,1,0:T(8,128)S(1)} reduce-window(s32[32,8,128]{2,1,0:T(8,128)S(1)} %fusion.25, s32[]{:T(128)} %constant.41.clone.1), window={size=1x1x128 pad=0_0x0_0x127_0}, to_apply=%region_0.0 | reduce-window | flops 4161536 | bytes 262148 | tf_op jit(solution)/shard_map/reduce-window
  17.5 0.1 slice.19
  17.6 0.1 copy.31
  17.8 0.1 copy.32
  17.8 0.1 add_add_fusion
  18.0 0.1 reduce_sum.30
  18.1 0.7 add_select_fusion
  18.8 2.2 select_reduce_fusion
  21.1 31.6 %all-gather.2.cloned.1.call-done = bf16[128,4096]{1,0:T(8,128)(2,1)} async-done(((bf16[128,512]{1,0:T(8,128)(2,1)}), bf16[128,4096]{1,0:T(8,128)(2,1)}) %all-gather.2.cloned.1.call-update) | async-done | bytes 1048592 | tf_op jit(solution)/shard_map/all_gather | solution.py:18
  52.7 1.9 convolution_convert_fusion
  54.6 0.0 copy-start.2
  54.6 100.8 %all_to_all.10 = bf16[16,16,4096]{2,1,0:T(8,128)(2,1)S(1)} all-to-all(bf16[16,16,4096]{2,1,0:T(8,128)(2,1)S(1)} %bitcast.55), channel_id=1, replica_groups=mesh['dp'=8,'ctx'=16,'tp'=8] {'ctx'}, dimensions={0} | all-to-all | bytes 4194304 | tf_op jit(solution)/shard_map/all_to_all | solution.py:42
  155.4 0.0 copy-start.1
  155.4 1.3 copy-done.1
  156.7 0.0 copy-done.2
  156.7 2.0 fusion.4
  158.8 0.0 copy-done
  158.8 6.3 %convolution_convert_fusion.1 = bf16[16,16,4096]{2,1,0:T(8,128)(2,1)} fusion(bf16[1,384,4096]{2,1,0:T(8,128)(2,1)S(1)} %copy-done, bf16[16,16,4096]{2,1,0:T(8,128)(2,1)} %copy-done.1, bf16[1,384,4096]{2,1,0:T(8,128)(2,1)} %param.12, f32[16,16,384]{2,1,0:T(8,128)} %fusion.4), kind=kOutput, calls=%fused_computation.1 | convolution fusion | flops 1612251136 | bytes 10878976 | tf_op jit(solution)/shard_map/scf,fd->scd/dot_general | solution.py:48
  165.1 103.2 %all_to_all.11 = bf16[16,16,4096]{2,1,0:T(8,128)(2,1)S(1)} all-to-all(bf16[16,16,4096]{2,1,0:T(8,128)(2,1)} %convolution_convert_fusion.1), channel_id=1, replica_groups=mesh['dp'=8,'ctx'=16,'tp'=8] {'ctx'}, dimensions={0} | all-to-all | bytes 4194304 | tf_op jit(solution)/shard_map/all_to_all | solution.py:50
  268.3 2.0 fusion
  270.3 0.0 reduce-scatter.2.cloned.1.call-update
  270.3 45.0 %reduce-scatter.2.cloned.1.call-done = bf16[128,512]{1,0:T(8,128)(2,1)} async-done(((bf16[128,4096]{1,0:T(8,128)(2,1)}), bf16[128,512]{1,0:T(8,128)(2,1)}) %reduce-scatter.2.cloned.1.call-update) | async-done | bytes 131088 | tf_op jit(solution)/shard_map/reduce_scatter | solution.py:57
  (6 shorter events, 0.2 us)
Async XLA Ops:
  6.5 152.2 %copy-start = (bf16[1,384,4096]{2,1,0:T(8,128)(2,1)S(1)}, bf16[1,384,4096]{2,1,0:T(8,128)(2,1)}, u32[]{:S(2)}) copy-start(bf16[1,384,4096]{2,1,0:T(8,128)(2,1)} %param.13) | copy-start | bytes 9437188
  6.5 46.1 %all-gather.2.cloned.1.call-start = ((), (), s32[]{:S(2)}) async-start(), calls=%async_computation.3 | async-start | bytes 1179648 | tf_op jit(solution)/shard_map/all_gather | solution.py:18
  7.3 308.1 %reduce-scatter.2.cloned.1.call-start = ((), (), s32[]{:S(2)}) async-start(), calls=%async_computation.4 | async-start | bytes 1179648 | tf_op jit(solution)/shard_map/reduce_scatter | solution.py:57
  54.6 102.1 %copy-start.2 = (bf16[1,384,4096]{2,1,0:T(8,128)(2,1)S(1)}, bf16[1,384,4096]{2,1,0:T(8,128)(2,1)}, u32[]{:S(2)}) copy-start(bf16[1,384,4096]{2,1,0:T(8,128)(2,1)} %param.11) | copy-start | bytes 9437188
  155.4 1.4 copy-start.1
Sparse Core Ops, SparseCore 0:
  10.1 42.5 all-gather.1
  270.4 44.8 reduce-scatter.1
where the time goes:
time: 322 us
  blocking collectives  204 us (63%)
  waiting for transfers between devices  77.4 us (24%)
  between operations  13.5 us (4%)
  matrix products  12.3 us (4%)
  other arithmetic  12.1 us (4%)
    all_to_all x1, blocking collectives, shards(): lax.all_to_all(part_out, 'ctx', split_axis=0, concat_axis=0, tiled=True)  103 us
    all_to_all x1, blocking collectives, shards(): lax.all_to_all(outgoing, 'ctx', split_axis=0, concat_axis=0, tiled=True)  101 us
    reduce_scatter x1, waiting for transfers between devices, shards(): lax.psum_scatter(term.astype(jnp.bfloat16), 'tp', scatter_dimension=1, ti...  45 us
    all_gather x1, waiting for transfers between devices, shards(): whole = lax.all_gather(tokens, 'tp', axis=1, tiled=True)  31.6 us
    another operation x2, other arithmetic  9.04 us
  transfers between devices with their start and end apart: 2, of which 2 were waited for; matrix products, arithmetic and copies ran while one was open for 4% of the time, Pallas kernels for 0%

commit v1 on v0

v1 whole, which is shorter than its diff:
```python
import jax
import jax.numpy as jnp
from jax import lax
from jax.experimental import pallas as pl
from jax.experimental.pallas import tpu as pltpu
from jax.sharding import PartitionSpec as P

MESH = pl.DeviceIdType.MESH
N = 16
CAP = 16
TOK = 128
TOP = 8
FS = 512
NS = 8
FQ = 384
NCH = 4
CB = N // NCH
CR = CB * CAP
DIST = [8, 7, 9, 6, 10, 5, 11, 4, 12, 3, 13, 2, 14, 1, 15, 0]
POS = {d: p for p, d in enumerate(DIST)}
BACK = [POS[(-d) % N] for d in DIST]


def kernel(tok, ids, rw, gate_h, up_h, down_h, out,
           xs, gate_v, up_v, down_v, pk, comb_hi, comb_lo, back, own, mate_s, mate_r, pair_s, pair_r, ret,
           wsem, zs, zr, xsend, xrecv, ms, mr, ps, pr, rs, rr):
    dp, c, t = lax.axis_index("dp"), lax.axis_index("ctx"), lax.axis_index("tp")
    x, k = t // 2, t % 2
    x2 = 3 - x
    xp = x + 1 - 2 * (x % 2)
    xp2 = 3 - xp
    t2 = 2 * x2 + k
    group = x // 2
    mate = 2 * x + 1 - k
    pair_same, pair_other = 2 * xp + k, 2 * xp + 1 - k

    def ctx_of(d):
        return lax.rem(c + d, N)

    def dev(cc, tt):
        return (dp, cc, tt)

    wcopies = [pltpu.make_async_copy(h, v, wsem.at[i])
               for i, (h, v) in enumerate(((gate_h, gate_v), (up_h, up_v), (down_h, down_v)))]
    for w in wcopies:
        w.start()

    barrier = pltpu.get_barrier_semaphore()
    peers = [dev(ctx_of(d), tt) for d in range(1, N) for tt in (t, t2)]
    peers += [dev(c, tt) for tt in (t2, mate, pair_same, pair_other)]
    for peer in peers:
        pl.semaphore_signal(barrier, inc=1, device_id=peer, device_id_type=MESH)

    place = lax.broadcasted_iota(jnp.int32, (2 * N, TOK), 0)
    expert = jnp.zeros((2 * N, TOK), jnp.int32)
    for p, d in enumerate(DIST):
        base = 2 * ctx_of(d)
        expert = jnp.where(place == 2 * p, base + group, expert)
        expert = jnp.where(place == 2 * p + 1, base + 1 - group, expert)
    marks = jnp.zeros((2 * N, TOK), jnp.float32)
    weight = jnp.zeros((2 * N, TOK), jnp.float32)
    for j in range(TOP):
        hit = ids[j:j + 1, :] == expert
        marks = jnp.where(hit, 1.0, marks)
        weight = jnp.where(hit, rw[j:j + 1, :], weight)
    row = lax.broadcasted_iota(jnp.int32, (TOK, TOK), 0)
    col = lax.broadcasted_iota(jnp.int32, (TOK, TOK), 1)
    above = jnp.where(row < col, 1.0, 0.0).astype(jnp.bfloat16)
    count = jnp.dot(marks.astype(jnp.bfloat16), above, preferred_element_type=jnp.float32)
    slot = jnp.where(marks > 0.0, count, -1.0)
    numbers = lax.broadcasted_iota(jnp.int32, (2 * N, CAP, TOK), 1).astype(jnp.float32)
    chosen = slot[:, None, :] == numbers
    pick = jnp.where(chosen, 1.0, 0.0).reshape(2 * N * CAP, TOK).astype(jnp.bfloat16)
    pk[...] = jnp.dot(pick, tok[...], preferred_element_type=jnp.float32).astype(jnp.bfloat16)

    pl.semaphore_wait(barrier, len(peers))

    def remote(src, dst, ssem, rsem, to):
        return pltpu.make_async_remote_copy(src_ref=src, dst_ref=dst, send_sem=ssem, recv_sem=rsem,
                                            device_id=to, device_id_type=MESH)

    pending = []

    for p, d in enumerate(DIST):
        q = BACK[p]
        for g, tt in ((0, t), (1, t2)):
            src = pk.at[pl.ds((2 * p + g) * CAP, CAP)]
            if d == 0 and g == 0:
                xs[t, q * CAP:(q + 1) * CAP, :] = src[...]
                continue
            cp = remote(src, xs.at[t, pl.ds(q * CAP, CAP)], zs.at[2 * p + g], zr.at[2 * q + g], dev(ctx_of(d), tt))
            cp.start()
            pending.append(cp)

    comb = jnp.where(chosen, weight[:, None, :], 0.0).reshape(2 * N * CAP, TOK).T
    hi = comb.astype(jnp.bfloat16)
    comb_hi[...] = hi
    comb_lo[...] = (comb - hi.astype(jnp.float32)).astype(jnp.bfloat16)

    def stage_a(j):
        rows = pl.ds(j * CR, CR)
        for p in range(j * CB, (j + 1) * CB):
            for g in range(2):
                if DIST[p] == 0 and g == 0:
                    continue
                dst = xs.at[t if g == 0 else t2, pl.ds(p * CAP, CAP)]
                remote(dst, dst, zs.at[2 * p + g], zr.at[2 * p + g], dev(c, mate)).wait_recv()
        for i, to in enumerate((pair_same, pair_other, mate)):
            for g, tt in ((0, t), (1, t2)):
                cp = remote(xs.at[tt, rows], xs.at[tt, rows], xsend.at[j, 2 * i + g], xrecv.at[j, 2 * i + g], dev(c, to))
                cp.start()
                pending.append(cp)

    def stage_b(j):
        rows = pl.ds(j * CR, CR)
        froms = ((2 * xp + k, 2 * xp2 + k), (2 * xp + 1 - k, 2 * xp2 + 1 - k), (2 * x + 1 - k, 2 * x2 + 1 - k))
        for i, slices in enumerate(froms):
            for g in range(2):
                dst = xs.at[slices[g], rows]
                remote(dst, dst, xsend.at[j, 2 * i + g], xrecv.at[j, 2 * i + g], dev(c, mate)).wait_recv()
        if j == 0:
            wcopies[0].wait()
            wcopies[1].wait()

        def gate_up(s, accs):
            g_acc, u_acc = accs
            a = xs[s, rows, :]
            cols = pl.ds(pl.multiple_of(s * FS, FS), FS)
            nt = (((1,), (1,)), ((), ()))
            g_acc = g_acc + lax.dot_general(a, gate_v[:, cols], nt, preferred_element_type=jnp.float32)
            u_acc = u_acc + lax.dot_general(a, up_v[:, cols], nt, preferred_element_type=jnp.float32)
            return g_acc, u_acc

        zero = jnp.zeros((CR, FQ), jnp.float32)
        g_acc, u_acc = lax.fori_loop(0, NS, gate_up, (zero, zero))
        hidden = (g_acc / (1.0 + jnp.exp(-g_acc)) * u_acc).astype(jnp.bfloat16)
        if j == 0:
            wcopies[2].wait()

        def down(s):
            cols = pl.ds(pl.multiple_of(s * FS, FS), FS)
            return jnp.dot(hidden, down_v[:, cols], preferred_element_type=jnp.float32)

        for xq in range(4):
            mate_s[j, xq] = down(2 * xq + 1 - k).astype(jnp.bfloat16)
        cp = remote(mate_s.at[j], mate_r.at[j], ms.at[j], mr.at[j], dev(c, mate))
        cp.start()
        pending.append(cp)
        for i, xq in enumerate((x, x2, xp, xp2)):
            own[j, i] = down(2 * xq + k)

    def stage_c(j):
        remote(mate_s.at[j], mate_r.at[j], ms.at[j], mr.at[j], dev(c, mate)).wait_recv()
        for i, xq in enumerate((xp, xp2)):
            pair_s[j, i] = (own[j, 2 + i] + mate_r[j, xq].astype(jnp.float32)).astype(jnp.bfloat16)
        cp = remote(pair_s.at[j], pair_r.at[j], ps.at[j], pr.at[j], dev(c, pair_same))
        cp.start()
        pending.append(cp)
        for i, xq in enumerate((x, x2)):
            own[j, i] = own[j, i] + mate_r[j, xq].astype(jnp.float32)

    def stage_d(j):
        remote(pair_s.at[j], pair_r.at[j], ps.at[j], pr.at[j], dev(c, pair_same)).wait_recv()
        for i in range(2):
            ret[j, i] = (own[j, i] + pair_r[j, i].astype(jnp.float32)).astype(jnp.bfloat16)
        for b in range(CB):
            p = j * CB + b
            q = BACK[p]
            for g, tt in ((0, t), (1, t2)):
                src = ret.at[j, g, pl.ds(b * CAP, CAP)]
                if DIST[p] == 0 and g == 0:
                    back[2 * q * CAP:(2 * q + 1) * CAP, :] = src[...]
                    continue
                cp = remote(src, back.at[pl.ds((2 * q + g) * CAP, CAP)], rs.at[2 * p + g], rr.at[2 * q + g],
                            dev(ctx_of(DIST[p]), tt))
                cp.start()
                pending.append(cp)

    for n in range(NCH + 3):
        if n < NCH:
            stage_a(n)
        if 0 <= n - 1 < NCH:
            stage_b(n - 1)
        if 0 <= n - 2 < NCH:
            stage_c(n - 2)
        if 0 <= n - 3 < NCH:
            stage_d(n - 3)

    total = None
    for j in range(NCH):
        for p in range(j * CB, (j + 1) * CB):
            for g in range(2):
                if DIST[p] == 0 and g == 0:
                    continue
                dst = back.at[pl.ds((2 * p + g) * CAP, CAP)]
                remote(dst, dst, rs.at[2 * p + g], rr.at[2 * p + g], dev(c, mate)).wait_recv()
        cols = slice(2 * j * CR, 2 * (j + 1) * CR)
        piece = back[cols, :]
        part = (jnp.dot(comb_hi[:, cols], piece, preferred_element_type=jnp.float32)
                + jnp.dot(comb_lo[:, cols], piece, preferred_element_type=jnp.float32))
        total = part if total is None else total + part
    out[...] = total.astype(jnp.bfloat16)
    for cp in pending:
        cp.wait_send()


def shards(tokens, expert_ids, route_weight, gate_weight, up_weight, down_weight):
    bf, f32 = jnp.bfloat16, jnp.float32
    vmem, dma = pltpu.VMEM, pltpu.SemaphoreType.DMA
    full = pl.BlockSpec(memory_space=pltpu.VMEM)
    hbm = pl.BlockSpec(memory_space=pl.ANY)
    return pl.pallas_call(
        kernel,
        out_shape=jax.ShapeDtypeStruct((TOK, FS), bf),
        in_specs=[full, full, full, hbm, hbm, hbm],
        out_specs=full,
        scratch_shapes=[
            vmem((NS, N * CAP, FS), bf),
            vmem((FQ, NS * FS), bf), vmem((FQ, NS * FS), bf), vmem((FQ, NS * FS), bf),
            vmem((2 * N * CAP, FS), bf), vmem((TOK, 2 * N * CAP), bf), vmem((TOK, 2 * N * CAP), bf),
            vmem((2 * N * CAP, FS), bf),
            vmem((NCH, 4, CR, FS), f32),
            vmem((NCH, 4, CR, FS), bf), vmem((NCH, 4, CR, FS), bf),
            vmem((NCH, 2, CR, FS), bf), vmem((NCH, 2, CR, FS), bf),
            vmem((NCH, 2, CR, FS), bf),
            dma((3,)), dma((2 * N,)), dma((2 * N,)), dma((NCH, 6)), dma((NCH, 6)),
            dma((NCH,)), dma((NCH,)), dma((NCH,)), dma((NCH,)), dma((2 * N,)), dma((2 * N,)),
        ],
        compiler_params=pltpu.CompilerParams(collective_id=0, has_side_effects=True, vmem_limit_bytes=60 << 20),
    )(tokens, expert_ids.T, route_weight.T, gate_weight[0], up_weight[0], down_weight[0])


def solution(mesh):
    return jax.shard_map(
        shards,
        mesh=mesh,
        in_specs=(
            P(("dp", "ctx"), "tp"),
            P(("dp", "ctx"), None),
            P(("dp", "ctx"), None),
            P(("ctx", "tp"), None, None),
            P(("ctx", "tp"), None, None),
            P(("ctx", "tp"), None, None),
        ),
        out_specs=P(("dp", "ctx"), "tp"),
        check_vma=False,
    )
```

time: 322 us -> 93.8 us (0.29)
  the two profiles are of different devices: /device:TPU:7 before, /device:TPU:3 now
where the time goes in v1:
time: 93.8 us; the launch traced here: 93.6 us
  Pallas kernels  92 us (98%)
  local copies, waits for them, and re-layouts  1.57 us (2%)
    pallas_call x1, Pallas kernels, shards(): pl.pallas_call(kernel, out_shape=jax.ShapeDtypeStruct((TOK, FS), bf), in_...  92 us

profile of v1, /device:TPU:3, one launch (start us, length us, event | category | flops | bytes accessed | tf_op | source)
XLA Modules:
  0.0 93.6 jit_solution(9514359482277744214)
XLA Ops:
  0.0 92.0 %shard_map.64 = bf16[128,512]{1,0:T(8,128)(2,1)} custom-call(bf16[128,512]{1,0:T(8,128)(2,1)} %tok.1, s32[8,128]{1,0:T(8,128)} %bitcast.8, f32[8,128]{1,0:T(8,128)} %bitcast.9, bf16[384,4096]{1,0:T(8,128)(2,1)} %bitcast.5, bf16[384,4096]{1,0:T(8,128)(2,1)} %bitcast.6, bf16[384,4096]{1,0:T(8,128)(2,1)} %bitcast.7), custom_call_target="tpu_custom_call" | custom-call | tf_op jit(solution)/shard_map/pallas_call | solution.py:212
  92.0 1.6 %copy.8 = bf16[128,512]{1,0:T(8,128)(2,1)} copy(bf16[128,512]{1,0:T(8,128)(2,1)} %shard_map.64) | data formatting | bytes 262144

commit v2 on v1

v2 whole, which is shorter than its diff:
```python
import jax
import jax.numpy as jnp
from jax import lax
from jax.experimental import pallas as pl
from jax.experimental.pallas import tpu as pltpu
from jax.sharding import PartitionSpec as P

MESH = pl.DeviceIdType.MESH
N = 16
CAP = 16
TOK = 128
TOP = 8
FS = 512
NS = 8
NX = 4
FQ = 384
SIZES = [4, 4, 4, 2, 2]
NCH = len(SIZES)
STARTS = [sum(SIZES[:j]) for j in range(NCH)]
DIST = [0, 8, 1, 15, 2, 14, 7, 9, 3, 13, 6, 10, 4, 12, 5, 11]
ORDER = ("A0", "S2", "A1", "S3", "F0", "B0", "F1", "C0", "A2", "S4", "B1", "D0",
         "A3", "F2", "C1", "B2", "D1", "A4", "F3", "C2", "B3", "D2", "F4", "C3",
         "B4", "D3", "C4", "D4")
POS = {d: p for p, d in enumerate(DIST)}
BACK = [POS[(-d) % N] for d in DIST]


def kernel(tok_h, ids_h, rw_h, gate_h, up_h, down_h, out,
           tok, ids, rw, zin, xs, gate_v, up_v, down_v, pk, comb_hi, comb_lo, back, own, mate_s, mate_r, chip_s, chip_r, ret,
           wsem, zs, zr, xsend, xrecv, fs, fr, ms, mr, ps, pr, rs, rr):
    dp, c, t = lax.axis_index("dp"), lax.axis_index("ctx"), lax.axis_index("tp")
    x, k = t // 2, t % 2
    group = t // 4
    mate = 2 * x + 1 - k

    def ctx_of(d):
        return lax.rem(c + d, N)

    def dev(cc, tt):
        return (dp, cc, tt)

    def chip(o):
        return lax.rem(x + o, NX)

    def local(h, v, i):
        return pltpu.make_async_copy(h, v, wsem.at[i])

    icopies = [local(ids_h, ids, 3), local(rw_h, rw, 4), local(tok_h, tok, 5)]
    for w in icopies:
        w.start()
    wcopies = [local(gate_h, gate_v, 0), local(up_h, up_v, 1), local(down_h, down_v, 2)]

    barrier = pltpu.get_barrier_semaphore()
    peers = [dev(ctx_of(d), t) for d in range(1, N)] + [dev(c, 2 * chip(o) + k) for o in range(1, NX)] + [dev(c, mate)]
    for peer in peers:
        pl.semaphore_signal(barrier, inc=1, device_id=peer, device_id_type=MESH)

    for w in icopies:
        w.wait()

    place = lax.broadcasted_iota(jnp.int32, (2 * N, TOK), 0)
    expert = jnp.zeros((2 * N, TOK), jnp.int32)
    for p, d in enumerate(DIST):
        expert = jnp.where(place == p, 2 * ctx_of(d), expert)
        expert = jnp.where(place == N + p, 2 * ctx_of(d) + 1, expert)
    marks = jnp.zeros((2 * N, TOK), jnp.float32)
    weight = jnp.zeros((2 * N, TOK), jnp.float32)
    for j in range(TOP):
        hit = ids[j:j + 1, :] == expert
        marks = jnp.where(hit, 1.0, marks)
        weight = jnp.where(hit, rw[j:j + 1, :], weight)
    row = lax.broadcasted_iota(jnp.int32, (TOK, TOK), 0)
    col = lax.broadcasted_iota(jnp.int32, (TOK, TOK), 1)
    above = jnp.where(row < col, 1.0, 0.0).astype(jnp.bfloat16)
    count = jnp.dot(marks.astype(jnp.bfloat16), above, preferred_element_type=jnp.float32)
    slot = jnp.where(marks > 0.0, count, -1.0)
    numbers = lax.broadcasted_iota(jnp.int32, (2 * N, CAP, TOK), 1).astype(jnp.float32)
    chosen = slot[:, None, :] == numbers

    def rows_of(j):
        return pl.ds(STARTS[j] * CAP, SIZES[j] * CAP)

    def blocks_of(j):
        return range(STARTS[j], STARTS[j] + SIZES[j])

    def pack(j):
        for g in range(2):
            first = g * N + STARTS[j]
            pick = jnp.where(chosen[first:first + SIZES[j]], 1.0, 0.0).reshape(SIZES[j] * CAP, TOK).astype(jnp.bfloat16)
            pk[g, rows_of(j), :] = jnp.dot(pick, tok[...], preferred_element_type=jnp.float32).astype(jnp.bfloat16)

    pack(0)
    pl.semaphore_wait(barrier, len(peers))

    def remote(src, dst, ssem, rsem, to):
        return pltpu.make_async_remote_copy(src_ref=src, dst_ref=dst, send_sem=ssem, recv_sem=rsem,
                                            device_id=to, device_id_type=MESH)

    pending = []

    def dispatch(j):
        for p in blocks_of(j):
            q, d = BACK[p], DIST[p]
            src, dst = pk.at[:, pl.ds(p * CAP, CAP)], zin.at[:, pl.ds(q * CAP, CAP)]
            if d == 0:
                dst[...] = src[...]
                continue
            cp = remote(src, dst, zs.at[p], zr.at[q], dev(ctx_of(d), t))
            cp.start()
            pending.append(cp)

    dispatch(0)
    pack(1)
    dispatch(1)
    for w in wcopies:
        w.start()
    for j in range(2, NCH):
        pack(j)
    comb = jnp.where(chosen, weight[:, None, :], 0.0).reshape(2 * N * CAP, TOK).T
    hi = comb.astype(jnp.bfloat16)
    comb_hi[...] = hi
    comb_lo[...] = (comb - hi.astype(jnp.float32)).astype(jnp.bfloat16)

    def stage_a(j):
        rows = rows_of(j)
        for p in blocks_of(j):
            if DIST[p] != 0:
                dst = zin.at[:, pl.ds(p * CAP, CAP)]
                remote(dst, dst, zs.at[p], zr.at[p], dev(ctx_of(1), t)).wait_recv()
        for o in (2, 1, 3):
            to = chip(o)
            cp = remote(zin.at[to // 2, rows], xs.at[k, x, rows], xsend.at[j, o], xrecv.at[j, o], dev(c, 2 * to + k))
            cp.start()
            pending.append(cp)
        xs[k, x, rows, :] = zin[group, rows, :]

    def stage_f(j):
        rows = rows_of(j)
        for o in (1, 3, 2):
            dst = xs.at[k, chip(NX - o), rows]
            remote(dst, dst, xsend.at[j, o], xrecv.at[j, o], dev(c, mate)).wait_recv()
        cp = remote(xs.at[k, :, rows], xs.at[k, :, rows], fs.at[j], fr.at[j], dev(c, mate))
        cp.start()
        pending.append(cp)

    def stage_b(j):
        rows = rows_of(j)
        if j == 0:
            wcopies[0].wait()
            wcopies[1].wait()

        def gate_up(parity):
            g_acc = u_acc = None
            nt = (((1,), (1,)), ((), ()))
            for xq in range(NX):
                a = xs[parity, xq, rows, :]
                cols = pl.ds(pl.multiple_of((2 * xq + parity) * FS, FS), FS)
                g_new = lax.dot_general(a, gate_v[:, cols], nt, preferred_element_type=jnp.float32)
                u_new = lax.dot_general(a, up_v[:, cols], nt, preferred_element_type=jnp.float32)
                g_acc = g_new if g_acc is None else g_acc + g_new
                u_acc = u_new if u_acc is None else u_acc + u_new
            return g_acc, u_acc

        g_mine, u_mine = gate_up(k)
        dst = xs.at[1 - k, :, rows]
        remote(dst, dst, fs.at[j], fr.at[j], dev(c, mate)).wait_recv()
        g_mate, u_mate = gate_up(1 - k)
        g_acc, u_acc = g_mine + g_mate, u_mine + u_mate
        hidden = (g_acc / (1.0 + jnp.exp(-g_acc)) * u_acc).astype(jnp.bfloat16)
        if j == 0:
            wcopies[2].wait()

        def down(xq, parity):
            cols = pl.ds(pl.multiple_of((2 * xq + parity) * FS, FS), FS)
            return jnp.dot(hidden, down_v[:, cols], preferred_element_type=jnp.float32)

        for xq in range(NX):
            mate_s[xq, rows, :] = down(xq, 1 - k).astype(jnp.bfloat16)
        cp = remote(mate_s.at[:, rows], mate_r.at[:, rows], ms.at[j], mr.at[j], dev(c, mate))
        cp.start()
        pending.append(cp)
        for o in range(NX):
            own[o, rows, :] = down(chip(o), k)

    def stage_c(j):
        rows = rows_of(j)
        remote(mate_s.at[:, rows], mate_r.at[:, rows], ms.at[j], mr.at[j], dev(c, mate)).wait_recv()
        for o in (2, 1, 3):
            to = chip(o)
            chip_s[o, rows, :] = (own[o, rows, :] + mate_r[to, rows, :].astype(jnp.float32)).astype(jnp.bfloat16)
            cp = remote(chip_s.at[o, rows], chip_r.at[x, rows], ps.at[j, o], pr.at[j, o], dev(c, 2 * to + k))
            cp.start()
            pending.append(cp)
        own[0, rows, :] = own[0, rows, :] + mate_r[x, rows, :].astype(jnp.float32)

    def stage_d(j):
        rows = rows_of(j)
        for o in (1, 3, 2):
            dst = chip_r.at[chip(NX - o), rows]
            remote(dst, dst, ps.at[j, o], pr.at[j, o], dev(c, mate)).wait_recv()
        pair = x + 1 - 2 * (x % 2)
        far = 2 * (1 - group)
        ret[group, rows, :] = (own[0, rows, :] + chip_r[pair, rows, :].astype(jnp.float32)).astype(jnp.bfloat16)
        ret[1 - group, rows, :] = (chip_r[far, rows, :].astype(jnp.float32)
                                   + chip_r[far + 1, rows, :].astype(jnp.float32)).astype(jnp.bfloat16)
        for p in blocks_of(j):
            q, d = BACK[p], DIST[p]
            src, dst = ret.at[:, pl.ds(p * CAP, CAP)], back.at[:, pl.ds(q * CAP, CAP)]
            if d == 0:
                dst[...] = src[...]
                continue
            cp = remote(src, dst, rs.at[p], rr.at[q], dev(ctx_of(d), t))
            cp.start()
            pending.append(cp)

    stages = {"A": stage_a, "F": stage_f, "B": stage_b, "C": stage_c, "D": stage_d, "S": dispatch}
    for step in ORDER:
        stages[step[0]](int(step[1]))

    total = None
    half = N // 2
    for h in range(2):
        for p in range(h * half, (h + 1) * half):
            if DIST[p] != 0:
                dst = back.at[:, pl.ds(p * CAP, CAP)]
                remote(dst, dst, rs.at[p], rr.at[p], dev(ctx_of(1), t)).wait_recv()
        for g in range(2):
            piece = back[g, h * half * CAP:(h + 1) * half * CAP, :]
            first = g * N * CAP + h * half * CAP
            cols = slice(first, first + half * CAP)
            part = (jnp.dot(comb_hi[:, cols], piece, preferred_element_type=jnp.float32)
                    + jnp.dot(comb_lo[:, cols], piece, preferred_element_type=jnp.float32))
            total = part if total is None else total + part
    out[...] = total.astype(jnp.bfloat16)
    for cp in pending:
        cp.wait_send()


def shards(tokens, expert_ids, route_weight, gate_weight, up_weight, down_weight):
    bf, f32 = jnp.bfloat16, jnp.float32
    vmem, dma = pltpu.VMEM, pltpu.SemaphoreType.DMA
    full = pl.BlockSpec(memory_space=pltpu.VMEM)
    hbm = pl.BlockSpec(memory_space=pltpu.HBM)
    return pl.pallas_call(
        kernel,
        out_shape=jax.ShapeDtypeStruct((TOK, FS), bf),
        in_specs=[hbm] * 6,
        out_specs=full,
        scratch_shapes=[
            vmem((TOK, FS), bf), vmem((TOP, TOK), jnp.int32), vmem((TOP, TOK), f32),
            vmem((2, N * CAP, FS), bf), vmem((2, NX, N * CAP, FS), bf),
            vmem((FQ, NS * FS), bf), vmem((FQ, NS * FS), bf), vmem((FQ, NS * FS), bf),
            vmem((2, N * CAP, FS), bf), vmem((TOK, 2 * N * CAP), bf), vmem((TOK, 2 * N * CAP), bf),
            vmem((2, N * CAP, FS), bf),
            vmem((NX, N * CAP, FS), f32),
            vmem((NX, N * CAP, FS), bf), vmem((NX, N * CAP, FS), bf),
            vmem((NX, N * CAP, FS), bf), vmem((NX, N * CAP, FS), bf), vmem((2, N * CAP, FS), bf),
            dma((6,)), dma((N,)), dma((N,)), dma((NCH, NX)), dma((NCH, NX)), dma((NCH,)), dma((NCH,)),
            dma((NCH,)), dma((NCH,)), dma((NCH, NX)), dma((NCH, NX)), dma((N,)), dma((N,)),
        ],
        compiler_params=pltpu.CompilerParams(collective_id=0, has_side_effects=True, vmem_limit_bytes=60 << 20),
    )(tokens, expert_ids.T, route_weight.T, gate_weight[0], up_weight[0], down_weight[0])


def solution(mesh):
    return jax.shard_map(
        shards,
        mesh=mesh,
        in_specs=(
            P(("dp", "ctx"), "tp"),
            P(("dp", "ctx"), None),
            P(("dp", "ctx"), None),
            P(("ctx", "tp"), None, None),
            P(("ctx", "tp"), None, None),
            P(("ctx", "tp"), None, None),
        ),
        out_specs=P(("dp", "ctx"), "tp"),
        check_vma=False,
    )
```

time: 93.8 us -> 78.5 us (0.84)
  the two profiles are of different devices: /device:TPU:3 before, /device:TPU:162 now
where the time goes in v2:
time: 78.5 us; the launch traced here: 78.3 us
  Pallas kernels  76.7 us (98%)
  local copies, waits for them, and re-layouts  1.57 us (2%)
    pallas_call x1, Pallas kernels, shards(): pl.pallas_call(kernel, out_shape=jax.ShapeDtypeStruct((TOK, FS), bf), in_...  76.7 us

profile of v2, /device:TPU:162, one launch (start us, length us, event | category | flops | bytes accessed | tf_op | source)
XLA Modules:
  0.0 78.3 jit_solution(11602244318607193292)
XLA Ops:
  0.0 76.7 %shard_map.64 = bf16[128,512]{1,0:T(8,128)(2,1)} custom-call(bf16[128,512]{1,0:T(8,128)(2,1)} %tok_h.1, s32[8,128]{1,0:T(8,128)} %bitcast.8, f32[8,128]{1,0:T(8,128)} %bitcast.9, bf16[384,4096]{1,0:T(8,128)(2,1)} %bitcast.5, bf16[384,4096]{1,0:T(8,128)(2,1)} %bitcast.6, bf16[384,4096]{1,0:T(8,128)(2,1)} %bitcast.7), custom_call_target="tpu_custom_call" | custom-call | tf_op jit(solution)/shard_map/pallas_call | solution.py:244
  76.7 1.6 %copy.8 = bf16[128,512]{1,0:T(8,128)(2,1)} copy(bf16[128,512]{1,0:T(8,128)(2,1)} %shard_map.64) | data formatting | bytes 262144

commit v3 on v2

--- a/solution.py
+++ b/solution.py
@@ -17,10 +17,10 @@
 SIZES = [4, 4, 4, 2, 2]
 NCH = len(SIZES)
 STARTS = [sum(SIZES[:j]) for j in range(NCH)]
-DIST = [0, 8, 1, 15, 2, 14, 7, 9, 3, 13, 6, 10, 4, 12, 5, 11]
-ORDER = ("A0", "S2", "A1", "S3", "F0", "B0", "F1", "C0", "A2", "S4", "B1", "D0",
-         "A3", "F2", "C1", "B2", "D1", "A4", "F3", "C2", "B3", "D2", "F4", "C3",
-         "B4", "D3", "C4", "D4")
+DIST = [0, 8, 2, 14, 1, 15, 7, 9, 3, 13, 6, 10, 4, 12, 5, 11]
+ORDER = ("A0", "S2", "X0", "A1", "S3", "X1", "F0", "B0", "F1", "C0", "A2", "S4",
+         "X2", "B1", "D0", "A3", "X3", "F2", "C1", "B2", "D1", "A4", "X4", "F3",
+         "C2", "B3", "D2", "F4", "C3", "B4", "D3", "C4", "D4")
 POS = {d: p for p, d in enumerate(DIST)}
 BACK = [POS[(-d) % N] for d in DIST]
 
@@ -122,16 +122,21 @@
     comb_lo[...] = (comb - hi.astype(jnp.float32)).astype(jnp.bfloat16)
 
     def stage_a(j):
-        rows = rows_of(j)
         for p in blocks_of(j):
             if DIST[p] != 0:
                 dst = zin.at[:, pl.ds(p * CAP, CAP)]
                 remote(dst, dst, zs.at[p], zr.at[p], dev(ctx_of(1), t)).wait_recv()
+
+    def stage_x(j):
+        rows = rows_of(j)
         for o in (2, 1, 3):
             to = chip(o)
             cp = remote(zin.at[to // 2, rows], xs.at[k, x, rows], xsend.at[j, o], xrecv.at[j, o], dev(c, 2 * to + k))
             cp.start()
             pending.append(cp)
+        cp = remote(zin.at[group, rows], xs.at[k, x, rows], fs.at[j, 0], fr.at[j, 0], dev(c, mate))
+        cp.start()
+        pending.append(cp)
         xs[k, x, rows, :] = zin[group, rows, :]
 
     def stage_f(j):
@@ -139,9 +144,9 @@
         for o in (1, 3, 2):
             dst = xs.at[k, chip(NX - o), rows]
             remote(dst, dst, xsend.at[j, o], xrecv.at[j, o], dev(c, mate)).wait_recv()
-        cp = remote(xs.at[k, :, rows], xs.at[k, :, rows], fs.at[j], fr.at[j], dev(c, mate))
-        cp.start()
-        pending.append(cp)
+            cp = remote(dst, dst, fs.at[j, o], fr.at[j, o], dev(c, mate))
+            cp.start()
+            pending.append(cp)
 
     def stage_b(j):
         rows = rows_of(j)
@@ -162,8 +167,9 @@
             return g_acc, u_acc
 
         g_mine, u_mine = gate_up(k)
-        dst = xs.at[1 - k, :, rows]
-        remote(dst, dst, fs.at[j], fr.at[j], dev(c, mate)).wait_recv()
+        for o in range(NX):
+            dst = xs.at[1 - k, chip(NX - o), rows]
+            remote(dst, dst, fs.at[j, o], fr.at[j, o], dev(c, mate)).wait_recv()
         g_mate, u_mate = gate_up(1 - k)
         g_acc, u_acc = g_mine + g_mate, u_mine + u_mate
         hidden = (g_acc / (1.0 + jnp.exp(-g_acc)) * u_acc).astype(jnp.bfloat16)
@@ -213,7 +219,7 @@
             cp.start()
             pending.append(cp)
 
-    stages = {"A": stage_a, "F": stage_f, "B": stage_b, "C": stage_c, "D": stage_d, "S": dispatch}
+    stages = {"A": stage_a, "X": stage_x, "F": stage_f, "B": stage_b, "C": stage_c, "D": stage_d, "S": dispatch}
     for step in ORDER:
         stages[step[0]](int(step[1]))
 
@@ -255,7 +261,7 @@
             vmem((NX, N * CAP, FS), f32),
             vmem((NX, N * CAP, FS), bf), vmem((NX, N * CAP, FS), bf),
             vmem((NX, N * CAP, FS), bf), vmem((NX, N * CAP, FS), bf), vmem((2, N * CAP, FS), bf),
-            dma((6,)), dma((N,)), dma((N,)), dma((NCH, NX)), dma((NCH, NX)), dma((NCH,)), dma((NCH,)),
+            dma((6,)), dma((N,)), dma((N,)), dma((NCH, NX)), dma((NCH, NX)), dma((NCH, NX)), dma((NCH, NX)),
             dma((NCH,)), dma((NCH,)), dma((NCH, NX)), dma((NCH, NX)), dma((N,)), dma((N,)),
         ],
         compiler_params=pltpu.CompilerParams(collective_id=0, has_side_effects=True, vmem_limit_bytes=60 << 20),

time: 78.5 us -> 78.4 us (level)
  the two profiles are of different devices: /device:TPU:162 before, /device:TPU:232 now
where the time goes in v3:
time: 78.4 us; the launch traced here: 78.3 us
  Pallas kernels  76.7 us (98%)
  local copies, waits for them, and re-layouts  1.57 us (2%)
    pallas_call x1, Pallas kernels, shards(): pl.pallas_call(kernel, out_shape=jax.ShapeDtypeStruct((TOK, FS), bf), in_...  76.7 us
    unnamed x1, local copies, waits for them, and re-layouts  1.57 us

profile of v3, /device:TPU:232, one launch (start us, length us, event | category | flops | bytes accessed | tf_op | source)
XLA Modules:
  0.0 78.3 jit_solution(12326352843264081291)
XLA Ops:
  0.0 76.7 %shard_map.64 = bf16[128,512]{1,0:T(8,128)(2,1)} custom-call(bf16[128,512]{1,0:T(8,128)(2,1)} %tok_h.1, s32[8,128]{1,0:T(8,128)} %bitcast.8, f32[8,128]{1,0:T(8,128)} %bitcast.9, bf16[384,4096]{1,0:T(8,128)(2,1)} %bitcast.5, bf16[384,4096]{1,0:T(8,128)(2,1)} %bitcast.6, bf16[384,4096]{1,0:T(8,128)(2,1)} %bitcast.7), custom_call_target="tpu_custom_call" | custom-call | tf_op jit(solution)/shard_map/pallas_call | solution.py:250
  76.7 1.6 %copy.8 = bf16[128,512]{1,0:T(8,128)(2,1)} copy(bf16[128,512]{1,0:T(8,128)(2,1)} %shard_map.64) | data formatting | bytes 262144
